TPU v7x, 32 devices: a whole 2x2x4 slice. The times are simulated.
32 devices in a mesh: mode: 4 (over y, x), space: 8 (over z, core).
Axes of the slice: x: 2, y: 2, z: 4, core: 2. Of those that a mesh axis runs over, the one named last changes fastest.
Arguments:
- modes: bfloat16 [64, 16, 64, 128], P('mode', 'space'), may hold values from -1.25 to 1.25
- regions: int32 [16, 64, 128], P('space'), may hold values from 0 to 7
- stiffness: float32 [8], replicated, may hold values from 0.05 to 4
- nonlinear: float32 [8], replicated, may hold values from 0.5 to 2
- plan: int32 [64, 3], P('mode'), may hold values from 0 to 15
Outputs:
- derivatives: float32 [64, 3, 16, 64, 128], P('mode', None, 'space')
All inputs are finite; a program needn't handle non-finite values.
Results may differ from a plain program's by a relative error of at most 0.0003.
Values may be sent and summed in bfloat16 or wider, within the bound.
A program may use at most 64 MiB of HBM per device.

v0:
```python
import jax
import jax.numpy as jnp
from jax import lax
from jax.sharding import PartitionSpec as P

PARTNERS = 3
ITERS = 3


mass_shift = 0.5


def with_halo(cells, sides, width):
    for axis, dim in sides:
        count = lax.axis_size(axis)
        ends = count - 1
        head = lax.slice_in_dim(cells, 0, width, axis=dim)
        tail = lax.slice_in_dim(cells, cells.shape[dim] - width, cells.shape[dim], axis=dim)
        cells = jnp.concatenate(
            [
                lax.ppermute(tail, axis, [(i, (i + 1) % count) for i in range(ends)]),
                cells,
                lax.ppermute(head, axis, [((i + 1) % count, i) for i in range(ends)]),
            ],
            axis=dim,
        )
    return cells


def from_behind(x, axis, by):
    devices = lax.axis_size(axis)
    return lax.ppermute(x, axis, [(i, (i + by) % devices) for i in range(devices)])


def laplace_core(ext):
    center = ext[:, 1:-1]
    padded = jnp.pad(center, ((0, 0), (0, 0), (1, 1), (1, 1)))
    beside = ext[:, 2:] + ext[:, :-2]
    beside = beside + padded[:, :, 2:, 1:-1] + padded[:, :, :-2, 1:-1]
    beside = beside + padded[:, :, 1:-1, 2:] + padded[:, :, 1:-1, :-2]
    return 6.0 * center - beside


def operate(field, weights, diag):
    lows_x, high_x, lows_y, high_y, lows_z, high_z = weights
    ext = with_halo(field, (("space", 1),), 1)
    padded = jnp.pad(field, ((0, 0), (0, 0), (1, 1), (1, 1)))
    out = diag * field - lows_x * ext[:, :-2] - high_x * ext[:, 2:]
    out = out - lows_y * padded[:, :, :-2, 1:-1] - high_y * padded[:, :, 2:, 1:-1]
    out = out - lows_z * padded[:, :, 1:-1, :-2] - high_z * padded[:, :, 1:-1, 2:]
    return out


def local_sum(left, right):
    return jnp.sum(left * right, axis=(1, 2, 3))


def pair_totals(residual, precond, image):
    return lax.psum((local_sum(residual, precond), local_sum(image, precond)), "space")


def expand(vector):
    return vector[:, None, None, None]


def shards(modes, regions, stiffness, nonlinear, plan):
    count = stiffness.shape[0]
    per_block = modes.shape[0]
    ids = with_halo(regions + 1, (("space", 0),), 1)
    labels = jnp.arange(1, count + 1, dtype=jnp.int32)[:, None, None, None]
    hits = (ids[None] == labels).astype(jnp.float32)
    coeff_ext = jnp.sum(hits * stiffness[:, None, None, None], 0)
    cubic_ext = jnp.sum(hits * nonlinear[:, None, None, None], 0)
    coeff = coeff_ext[1:-1]
    cpad = jnp.pad(coeff, ((0, 0), (1, 1), (1, 1)))
    lows_x = 0.5 * (coeff + coeff_ext[:-2])
    high_x = 0.5 * (coeff + coeff_ext[2:])
    lows_y = 0.5 * (coeff + cpad[:, :-2, 1:-1])
    high_y = 0.5 * (coeff + cpad[:, 2:, 1:-1])
    lows_z = 0.5 * (coeff + cpad[:, 1:-1, :-2])
    high_z = 0.5 * (coeff + cpad[:, 1:-1, 2:])
    weights = (lows_x, high_x, lows_y, high_y, lows_z, high_z)
    diag = mass_shift + lows_x + high_x + lows_y + high_y + lows_z + high_z
    blocks = [modes]
    carried = modes
    for step in range(PARTNERS - 1):
        carried = from_behind(carried, "mode", 1)
        blocks.append(carried)
    stacked = jnp.concatenate(blocks, 0)
    places = jnp.arange(per_block, dtype=jnp.int32)
    ext = with_halo(stacked, (("space", 1),), 1)
    lap = laplace_core(ext.astype(jnp.float32))
    own = lap[:per_block]
    chosen = []
    for s in range(PARTNERS):
        select = (plan[:, s][:, None] == places[None]).astype(jnp.float32)
        chosen.append(
            jnp.einsum(
                "ab,bxyz->axyz",
                select,
                lap[s * per_block : (s + 1) * per_block],
                precision=lax.Precision.HIGHEST,
            )
        )
    own, chosen = (own, jnp.stack(chosen, 1))
    product = cubic_ext[1:-1] * own[:, None] * chosen
    product = product.reshape((per_block * PARTNERS,) + product.shape[2:])
    ext_prod = with_halo(product, (("space", 1),), 1)
    rhs = -laplace_core(ext_prod)
    solution = jnp.zeros_like(rhs)
    residual = rhs
    precond = residual / diag
    image = operate(precond, weights, diag)
    gamma, delta = pair_totals(residual, precond, image)
    alpha = gamma / delta
    direction, along = (precond, image)
    for step in range(ITERS):
        solution = solution + expand(alpha) * direction
        residual = residual - expand(alpha) * along
        if step + 1 < ITERS:
            precond = residual / diag
            image = operate(precond, weights, diag)
            gamma_next, delta = pair_totals(residual, precond, image)
            ratio = gamma_next / gamma
            alpha = gamma_next / (delta - ratio * gamma_next / alpha)
            direction = precond + expand(ratio) * direction
            along = image + expand(ratio) * along
            gamma = gamma_next
    return solution.reshape((per_block, PARTNERS) + solution.shape[1:])


def solution(mesh):
    return jax.shard_map(
        shards,
        mesh=mesh,
        in_specs=(
            P("mode", "space", None, None),
            P("space", None, None),
            P(),
            P(),
            P("mode", None),
        ),
        out_specs=P("mode", None, "space", None, None),
        check_vma=False,
    )
```

profile of v0, /device:TPU:0, one launch (start us, length us, event | category | flops | bytes accessed | tf_op | source)
XLA Modules:
  0.0 226.3 jit_solution(2418801493072548243)
XLA Ops:
  0.0 1.4 fusion.89
  1.5 3.0 %collective-permute-start.2 = (bf16[16,2,64,128]{3,0,2,1:T(8,128)(2,1)S(1)}, bf16[16,2,64,128]{3,0,2,1:T(8,128)(2,1)S(1)}, u32[]{:S(2)}, u32[]{:S(2)}) collective-permute-start(bf16[16,2,64,128]{3,0,2,1:T(8,128)(2,1)S(1)} %get-tuple-element.47), channel_id=1, source_target_pairs={{0,8},{8,16},{16,24},{24,0},{1,9},{9,17},{17,25},{25,1},{2,10},{10... | collective-permute-start | bytes 1572872 | tf_op jit(solution)/shard_map/ppermute | solution.py:32
  4.5 12.9 %collective-permute-done.2 = bf16[16,2,64,128]{3,0,2,1:T(8,128)(2,1)S(1)} collective-permute-done((bf16[16,2,64,128]{3,0,2,1:T(8,128)(2,1)S(1)}, bf16[16,2,64,128]{3,0,2,1:T(8,128)(2,1)S(1)}, u32[]{:S(2)}, u32[]{:S(2)}) %collective-permute-start.2) | collective-permute-done | bytes 524320 | tf_op jit(solution)/shard_map/ppermute | solution.py:32
  19.1 12.3 %collective-permute-done.3 = bf16[16,2,64,128]{3,0,2,1:T(8,128)(2,1)S(1)} collective-permute-done((bf16[16,2,64,128]{3,0,2,1:T(8,128)(2,1)S(1)}, bf16[16,2,64,128]{3,0,2,1:T(8,128)(2,1)S(1)}, u32[]{:S(2)}, u32[]{:S(2)}) %collective-permute-start.3) | collective-permute-done | bytes 524320 | tf_op jit(solution)/shard_map/ppermute | solution.py:32
  34.2 4.7 %collective-permute-start = (s32[1,64,128]{2,1,0:T(8,128)S(1)}, s32[1,64,128]{2,1,0:T(8,128)S(1)}, u32[]{:S(2)}, u32[]{:S(2)}) collective-permute-start(s32[1,64,128]{2,1,0:T(8,128)S(1)} %get-tuple-element.49), channel_id=1, source_target_pairs={{0,1},{1,2},{2,3},{3,4},{4,5},{5,6},{6,7},{8,9},{9,10},{10,11},{11... | collective-permute-start | bytes 98312 | tf_op jit(solution)/shard_map/ppermute | solution.py:21
  40.2 3.0 %collective-permute-done.1 = s32[1,64,128]{2,1,0:T(8,128)S(1)} collective-permute-done((s32[1,64,128]{2,1,0:T(8,128)S(1)}, s32[1,64,128]{2,1,0:T(8,128)S(1)}, u32[]{:S(2)}, u32[]{:S(2)}) %collective-permute-start.1) | collective-permute-done | bytes 32800 | tf_op jit(solution)/shard_map/ppermute | solution.py:23
  44.3 2.0 fusion.4
  49.6 1.8 copy.23
  53.0 8.1 %collective-permute-start.7 = (f32[48,1,64,128]{3,0,2,1:T(8,128)S(1)}, f32[48,1,64,128]{3,0,2,1:T(8,128)S(1)}, u32[]{:S(2)}, u32[]{:S(2)}) collective-permute-start(f32[48,1,64,128]{3,0,2,1:T(8,128)S(1)} %get-tuple-element.44), channel_id=1, source_target_pairs={{0,1},{1,2},{2,3},{3,4},{4,5},{5,6},{6,7},{8,9},{9,10},{10,11},{11... | collective-permute-start | bytes 4718600 | tf_op jit(solution)/shard_map/ppermute | solution.py:21
  61.9 2.1 collective-permute-done.7
  64.0 2.2 broadcast_divide_fusion.2
  66.4 18.1 %collective-permute-start.8 = (f32[48,1,64,128]{3,0,2,1:T(8,128)S(1)}, f32[48,1,64,128]{3,0,2,1:T(8,128)S(1)}, u32[]{:S(2)}, u32[]{:S(2)}) collective-permute-start(f32[48,1,64,128]{3,0,2,1:T(8,128)S(1)} %get-tuple-element.41), channel_id=1, source_target_pairs={{0,1},{1,2},{2,3},{3,4},{4,5},{5,6},{6,7},{8,9},{9,10},{10,11},{11... | collective-permute-start | bytes 4718600 | tf_op jit(solution)/shard_map/ppermute | solution.py:21
  84.5 1.5 collective-permute-start.9
  86.0 1.4 collective-permute-done.8
  87.4 4.3 %collective-permute-done.9 = f32[48,1,64,128]{3,0,2,1:T(8,128)S(1)} collective-permute-done((f32[48,1,64,128]{3,0,2,1:T(8,128)S(1)}, f32[48,1,64,128]{3,0,2,1:T(8,128)S(1)}, u32[]{:S(2)}, u32[]{:S(2)}) %collective-permute-start.9) | collective-permute-done | bytes 1572896 | tf_op jit(solution)/shard_map/ppermute | solution.py:23
  91.7 5.6 %multiply_reduce_fusion.3 = (f32[48]{0:T(128)S(1)}, f32[48]{0:T(128)S(1)}, f32[48,2,64,128]{3,0,2,1:T(8,128)}) fusion(f32[48,2,64,128]{3,0,2,1:T(8,128)S(1)} %get-tuple-element.29, f32[2,64,128]{2,1,0:T(8,128)S(1)} %get-tuple-element.30, f32[2,64,128]{2,1,0:T(8,128)S(1)} %get-tuple-element.36, f32[2,64,128]{2,1,0:T(8,128)S(1)} %get-tuple-element.35, ...), kind=kLoop, calls=%fused_computation.86 | loop fusion | flops 15728544 | bytes 13042048 | tf_op jit(solution)/shard_map/reduce_sum | solution.py:55
  97.3 30.5 %all-reduce.8 = (f32[48]{0:T(128)S(1)}, f32[48]{0:T(128)S(1)}) all-reduce(f32[48]{0:T(128)S(1)} %get-tuple-element.6, f32[48]{0:T(128)S(1)} %get-tuple-element.5), channel_id=1, replica_groups=mesh['mode'=4,'space'=8] {'space'}, use_global_device_ids=true, to_apply=%region_3.4 | all-reduce | flops 96 | bytes 768 | tf_op jit(solution)/shard_map/psum | solution.py:59
  127.8 2.4 %broadcast_divide_fusion.1 = f32[48,2,64,128]{3,0,2,1:T(8,128)S(1)} fusion(f32[2,64,128]{2,1,0:T(8,128)S(1)} %get-tuple-element.30, f32[48,2,64,128]{3,0,2,1:T(8,128)S(1)} %get-tuple-element.29, f32[48,2,64,128]{3,0,2,1:T(8,128)} %get-tuple-element.27, f32[48]{0:T(128)S(1)} %div.43), kind=kLoop, calls=%fused_computation.90 | loop fusion | flops 2359296 | bytes 9502912 | tf_op jit(solution)/shard_map/div | solution.py:121
  130.5 1.7 collective-permute-start.10
  132.2 1.4 collective-permute-start.11
  133.6 1.5 collective-permute-done.10
  135.1 2.5 %collective-permute-done.11 = f32[48,1,64,128]{3,0,2,1:T(8,128)S(1)} collective-permute-done((f32[48,1,64,128]{3,0,2,1:T(8,128)S(1)}, f32[48,1,64,128]{3,0,2,1:T(8,128)S(1)}, u32[]{:S(2)}, u32[]{:S(2)}) %collective-permute-start.11) | collective-permute-done | bytes 1572896 | tf_op jit(solution)/shard_map/ppermute | solution.py:23
  137.6 5.8 %multiply_reduce_fusion.1 = (f32[48]{0:T(128)S(1)}, f32[48]{0:T(128)S(1)}, f32[48,2,64,128]{3,0,2,1:T(8,128)}) fusion(f32[48,2,64,128]{3,0,2,1:T(8,128)S(1)} %broadcast_divide_fusion.1, f32[48,2,64,128]{3,0,2,1:T(8,128)S(1)} %get-tuple-element.29, f32[48,2,64,128]{3,0,2,1:T(8,128)S(1)} %copy-done.1, f32[48]{0:T(128)S(1)} %div.43, ...), kind=kLoop, calls=%fused_computation.83 | loop fusion | flops 16514976 | bytes 16187968 | tf_op jit(solution)/shard_map/reduce_sum | solution.py:55
  143.4 29.4 %all-reduce.7 = (f32[48]{0:T(128)S(1)}, f32[48]{0:T(128)}) all-reduce(f32[48]{0:T(128)S(1)} %get-tuple-element.8, f32[48]{0:T(128)S(1)} %get-tuple-element.7), channel_id=1, replica_groups=mesh['mode'=4,'space'=8] {'space'}, use_global_device_ids=true, to_apply=%region_7.8 | all-reduce | flops 96 | bytes 768 | tf_op jit(solution)/shard_map/psum | solution.py:59
  174.0 3.7 %broadcast_divide_fusion = (f32[48,2,64,128]{3,0,2,1:T(8,128)S(1)}, f32[48,2,64,128]{3,0,2,1:T(8,128)S(1)}) fusion(f32[2,64,128]{2,1,0:T(8,128)S(1)} %get-tuple-element.30, f32[48,2,64,128]{3,0,2,1:T(8,128)} %get-tuple-element.26, f32[48,2,64,128]{3,0,2,1:T(8,128)} %get-tuple-element.27, f32[48]{0:T(128)S(1)} %get-tuple-element.25, ...), kind=kLoop, calls=%fused_computation.89 | loop fusion | flops 5505024 | bytes 15794752 | tf_op jit(solution)/shard_map/div | solution.py:121
  178.0 1.4 collective-permute-start.12
  180.7 1.6 collective-permute-done.12
  182.3 2.4 %collective-permute-done.13 = f32[48,1,64,128]{3,0,2,1:T(8,128)S(1)} collective-permute-done((f32[48,1,64,128]{3,0,2,1:T(8,128)S(1)}, f32[48,1,64,128]{3,0,2,1:T(8,128)S(1)}, u32[]{:S(2)}, u32[]{:S(2)}) %collective-permute-start.13) | collective-permute-done | bytes 1572896 | tf_op jit(solution)/shard_map/ppermute | solution.py:23
  184.7 5.3 %fusion.49 = (f32[48]{0:T(128)}, f32[48]{0:T(128)}) fusion(f32[48,2,64,128]{3,0,2,1:T(8,128)S(1)} %get-tuple-element.21, f32[48,1,64,128]{3,0,2,1:T(8,128)S(1)} %collective-permute-done.13, f32[48,1,64,128]{3,0,2,1:T(8,128)S(1)} %collective-permute-done.12, f32[2,64,128]{2,1,0:T(8,128)S(1)} %copy-done.5, f32[2,64,128]{2,1,0:T(8,128)S(1)} %get-tuple-element.35, ...), kind=kLoop, calls=%fused_computation.88 | loop fusion | flops 15728544 | bytes 9896320 | tf_op jit(solution)/shard_map/reduce_sum | solution.py:55
  190.1 28.8 %all-reduce.6 = (f32[48]{0:T(128)S(1)}, f32[48]{0:T(128)S(1)}) all-reduce(f32[48]{0:T(128)} %get-tuple-element.12, f32[48]{0:T(128)} %get-tuple-element.11), channel_id=1, replica_groups=mesh['mode'=4,'space'=8] {'space'}, use_global_device_ids=true, to_apply=%region_11.12 | all-reduce | flops 96 | bytes 768 | tf_op jit(solution)/shard_map/psum | solution.py:59
  219.5 4.1 %multiply_add_fusion = f32[48,2,64,128]{3,0,2,1:T(8,128)S(1)} fusion(f32[48,2,64,128]{3,0,2,1:T(8,128)} %copy-done, f32[48]{0:T(128)S(1)} %get-tuple-element.20, f32[48]{0:T(128)S(1)} %get-tuple-element.19, f32[48]{0:T(128)S(1)} %get-tuple-element.25, f32[48]{0:T(128)S(1)} %get-tuple-element.23, f32[48]{0:T(128)S(1)} %div.43, ...), kind=kLoop, calls=%fused_computation.80 | loop fusion | flops 8650752 | bytes 12649408 | tf_op jit(solution)/shard_map/add | solution.py:118
  223.6 2.6 %copy.29 = f32[48,2,64,128]{3,2,1,0:T(8,128)} copy(f32[48,2,64,128]{3,0,2,1:T(8,128)S(1)} %multiply_add_fusion) | data formatting | bytes 6291456 | tf_op jit(solution)/shard_map/add | solution.py:118
  (59 shorter events, 16.2 us)
Async XLA Ops:
  1.4 38.7 %copy-start.6 = (s32[16,3]{0,1:T(4,128)S(1)}, s32[16,3]{0,1:T(4,128)}, u32[]{:S(2)}) copy-start(s32[16,3]{0,1:T(4,128)} %param.9) | copy-start | bytes 580
  1.5 41.8 %copy-start.7 = (f32[8]{0:T(128)S(1)}, f32[8]{0:T(128)}, u32[]{:S(2)}) copy-start(f32[8]{0:T(128)} %param.8) | copy-start | bytes 100
  1.5 41.8 %copy-start.8 = (f32[8]{0:T(128)S(1)}, f32[8]{0:T(128)}, u32[]{:S(2)}) copy-start(f32[8]{0:T(128)} %param.7) | copy-start | bytes 100
  1.5 15.9 %collective-permute-start.2 = (bf16[16,2,64,128]{3,0,2,1:T(8,128)(2,1)S(1)}, bf16[16,2,64,128]{3,0,2,1:T(8,128)(2,1)S(1)}, u32[]{:S(2)}, u32[]{:S(2)}) collective-permute-start(bf16[16,2,64,128]{3,0,2,1:T(8,128)(2,1)S(1)} %get-tuple-element.47), channel_id=1, source_target_pairs={{0,8},{8,16},{16,24},{24,0},{1,9},{9,17},{17,25},{25,1},{2,10},{10... | collective-permute-start | bytes 1572872 | tf_op jit(solution)/shard_map/ppermute | solution.py:32
  17.4 14.0 %collective-permute-start.3 = (bf16[16,2,64,128]{3,0,2,1:T(8,128)(2,1)S(1)}, bf16[16,2,64,128]{3,0,2,1:T(8,128)(2,1)S(1)}, u32[]{:S(2)}, u32[]{:S(2)}) collective-permute-start(bf16[16,2,64,128]{3,0,2,1:T(8,128)(2,1)S(1)} %collective-permute-done.2), channel_id=1, source_target_pairs={{0,8},{8,16},{16,24},{24,0},{1,9},{9,17},{17,25},{25,1},{2,10},{10... | collective-permute-start | bytes 1572872 | tf_op jit(solution)/shard_map/ppermute | solution.py:32
  31.5 12.0 %collective-permute-start.4 = (bf16[48,1,64,128]{3,0,2,1:T(8,128)(2,1)S(1)}, bf16[48,1,64,128]{3,0,2,1:T(8,128)(2,1)S(1)}, u32[]{:S(2)}, u32[]{:S(2)}) collective-permute-start(bf16[48,1,64,128]{3,0,2,1:T(8,128)(2,1)S(1)} %get-tuple-element.45), channel_id=1, source_target_pairs={{0,1},{1,2},{2,3},{3,4},{4,5},{5,6},{6,7},{8,9},{9,10},{10,11},{11... | collective-permute-start | bytes 2359304 | tf_op jit(solution)/shard_map/ppermute | solution.py:21
  32.9 10.6 %collective-permute-start.5 = (bf16[48,1,64,128]{3,0,2,1:T(8,128)(2,1)S(1)}, bf16[48,1,64,128]{3,0,2,1:T(8,128)(2,1)S(1)}, u32[]{:S(2)}, u32[]{:S(2)}) collective-permute-start(bf16[48,1,64,128]{3,0,2,1:T(8,128)(2,1)S(1)} %get-tuple-element.46), channel_id=1, source_target_pairs={{1,0},{2,1},{3,2},{4,3},{5,4},{6,5},{7,6},{9,8},{10,9},{11,10},{12... | collective-permute-start | bytes 2359304 | tf_op jit(solution)/shard_map/ppermute | solution.py:23
  34.2 6.0 %collective-permute-start = (s32[1,64,128]{2,1,0:T(8,128)S(1)}, s32[1,64,128]{2,1,0:T(8,128)S(1)}, u32[]{:S(2)}, u32[]{:S(2)}) collective-permute-start(s32[1,64,128]{2,1,0:T(8,128)S(1)} %get-tuple-element.49), channel_id=1, source_target_pairs={{0,1},{1,2},{2,3},{3,4},{4,5},{5,6},{6,7},{8,9},{9,10},{10,11},{11... | collective-permute-start | bytes 98312 | tf_op jit(solution)/shard_map/ppermute | solution.py:21
  38.9 4.3 %collective-permute-start.1 = (s32[1,64,128]{2,1,0:T(8,128)S(1)}, s32[1,64,128]{2,1,0:T(8,128)S(1)}, u32[]{:S(2)}, u32[]{:S(2)}) collective-permute-start(s32[1,64,128]{2,1,0:T(8,128)S(1)} %get-tuple-element.50), channel_id=1, source_target_pairs={{1,0},{2,1},{3,2},{4,3},{5,4},{6,5},{7,6},{9,8},{10,9},{11,10},{12... | collective-permute-start | bytes 98312 | tf_op jit(solution)/shard_map/ppermute | solution.py:23
  51.7 10.3 %collective-permute-start.6 = (f32[48,1,64,128]{3,0,2,1:T(8,128)S(1)}, f32[48,1,64,128]{3,0,2,1:T(8,128)S(1)}, u32[]{:S(2)}, u32[]{:S(2)}) collective-permute-start(f32[48,1,64,128]{3,0,2,1:T(8,128)S(1)} %get-tuple-element.43), channel_id=1, source_target_pairs={{1,0},{2,1},{3,2},{4,3},{5,4},{6,5},{7,6},{9,8},{10,9},{11,10},{12... | collective-permute-start | bytes 4718600 | tf_op jit(solution)/shard_map/ppermute | solution.py:23
  53.0 11.0 %collective-permute-start.7 = (f32[48,1,64,128]{3,0,2,1:T(8,128)S(1)}, f32[48,1,64,128]{3,0,2,1:T(8,128)S(1)}, u32[]{:S(2)}, u32[]{:S(2)}) collective-permute-start(f32[48,1,64,128]{3,0,2,1:T(8,128)S(1)} %get-tuple-element.44), channel_id=1, source_target_pairs={{0,1},{1,2},{2,3},{3,4},{4,5},{5,6},{6,7},{8,9},{9,10},{10,11},{11... | collective-permute-start | bytes 4718600 | tf_op jit(solution)/shard_map/ppermute | solution.py:21
  61.2 30.5 %copy-start.3 = (f32[2,64,128]{2,1,0:T(8,128)}, f32[2,64,128]{2,1,0:T(8,128)S(1)}, u32[]{:S(2)}) copy-start(f32[2,64,128]{2,1,0:T(8,128)S(1)} %get-tuple-element.36) | copy-start | bytes 196612
  66.4 21.0 %collective-permute-start.8 = (f32[48,1,64,128]{3,0,2,1:T(8,128)S(1)}, f32[48,1,64,128]{3,0,2,1:T(8,128)S(1)}, u32[]{:S(2)}, u32[]{:S(2)}) collective-permute-start(f32[48,1,64,128]{3,0,2,1:T(8,128)S(1)} %get-tuple-element.41), channel_id=1, source_target_pairs={{0,1},{1,2},{2,3},{3,4},{4,5},{5,6},{6,7},{8,9},{9,10},{10,11},{11... | collective-permute-start | bytes 4718600 | tf_op jit(solution)/shard_map/ppermute | solution.py:21
  84.5 7.2 %collective-permute-start.9 = (f32[48,1,64,128]{3,0,2,1:T(8,128)S(1)}, f32[48,1,64,128]{3,0,2,1:T(8,128)S(1)}, u32[]{:S(2)}, u32[]{:S(2)}) collective-permute-start(f32[48,1,64,128]{3,0,2,1:T(8,128)S(1)} %get-tuple-element.42), channel_id=1, source_target_pairs={{1,0},{2,1},{3,2},{4,3},{5,4},{6,5},{7,6},{9,8},{10,9},{11,10},{12... | collective-permute-start | bytes 4718600 | tf_op jit(solution)/shard_map/ppermute | solution.py:23
  127.8 2.4 %copy-start.9 = (f32[48]{0:T(128)}, f32[48]{0:T(128)S(1)}, u32[]{:S(2)}) copy-start(f32[48]{0:T(128)S(1)} %get-tuple-element.17) | copy-start | bytes 580
  127.8 2.5 %copy-start.10 = (f32[48]{0:T(128)}, f32[48]{0:T(128)S(1)}, u32[]{:S(2)}) copy-start(f32[48]{0:T(128)S(1)} %get-tuple-element.18) | copy-start | bytes 580
  130.3 7.3 %copy-start = (f32[48,2,64,128]{3,0,2,1:T(8,128)}, f32[48,2,64,128]{3,0,2,1:T(8,128)S(1)}, u32[]{:S(2)}) copy-start(f32[48,2,64,128]{3,0,2,1:T(8,128)S(1)} %broadcast_divide_fusion.1) | copy-start | bytes 9437188
  130.3 7.3 %copy-start.1 = (f32[48,2,64,128]{3,0,2,1:T(8,128)S(1)}, f32[48,2,64,128]{3,0,2,1:T(8,128)}, u32[]{:S(2)}) copy-start(f32[48,2,64,128]{3,0,2,1:T(8,128)} %get-tuple-element.27) | copy-start | bytes 9437188
  130.3 7.3 %copy-start.4 = (f32[2,64,128]{2,1,0:T(8,128)S(1)}, f32[2,64,128]{2,1,0:T(8,128)}, u32[]{:S(2)}) copy-start(f32[2,64,128]{2,1,0:T(8,128)} %copy-done.3) | copy-start | bytes 196612
  130.5 4.6 %collective-permute-start.10 = (f32[48,1,64,128]{3,0,2,1:T(8,128)S(1)}, f32[48,1,64,128]{3,0,2,1:T(8,128)S(1)}, u32[]{:S(2)}, u32[]{:S(2)}) collective-permute-start(f32[48,1,64,128]{3,0,2,1:T(8,128)S(1)} %get-tuple-element.39), channel_id=1, source_target_pairs={{0,1},{1,2},{2,3},{3,4},{4,5},{5,6},{6,7},{8,9},{9,10},{10,11},{11... | collective-permute-start | bytes 4718600 | tf_op jit(solution)/shard_map/ppermute | solution.py:21
  132.2 5.4 %collective-permute-start.11 = (f32[48,1,64,128]{3,0,2,1:T(8,128)S(1)}, f32[48,1,64,128]{3,0,2,1:T(8,128)S(1)}, u32[]{:S(2)}, u32[]{:S(2)}) collective-permute-start(f32[48,1,64,128]{3,0,2,1:T(8,128)S(1)} %get-tuple-element.40), channel_id=1, source_target_pairs={{1,0},{2,1},{3,2},{4,3},{5,4},{6,5},{7,6},{9,8},{10,9},{11,10},{12... | collective-permute-start | bytes 4718600 | tf_op jit(solution)/shard_map/ppermute | solution.py:23
  177.8 6.9 %copy-start.2 = (f32[48,2,64,128]{3,0,2,1:T(8,128)}, f32[48,2,64,128]{3,0,2,1:T(8,128)S(1)}, u32[]{:S(2)}) copy-start(f32[48,2,64,128]{3,0,2,1:T(8,128)S(1)} %get-tuple-element.22) | copy-start | bytes 9437188
  177.8 6.9 %copy-start.5 = (f32[2,64,128]{2,1,0:T(8,128)S(1)}, f32[2,64,128]{2,1,0:T(8,128)}, u32[]{:S(2)}) copy-start(f32[2,64,128]{2,1,0:T(8,128)} %copy-done.3) | copy-start | bytes 196612
  178.0 4.3 %collective-permute-start.12 = (f32[48,1,64,128]{3,0,2,1:T(8,128)S(1)}, f32[48,1,64,128]{3,0,2,1:T(8,128)S(1)}, u32[]{:S(2)}, u32[]{:S(2)}) collective-permute-start(f32[48,1,64,128]{3,0,2,1:T(8,128)S(1)} %get-tuple-element.37), channel_id=1, source_target_pairs={{0,1},{1,2},{2,3},{3,4},{4,5},{5,6},{6,7},{8,9},{9,10},{10,11},{11... | collective-permute-start | bytes 4718600 | tf_op jit(solution)/shard_map/ppermute | solution.py:21
  179.4 5.3 %collective-permute-start.13 = (f32[48,1,64,128]{3,0,2,1:T(8,128)S(1)}, f32[48,1,64,128]{3,0,2,1:T(8,128)S(1)}, u32[]{:S(2)}, u32[]{:S(2)}) collective-permute-start(f32[48,1,64,128]{3,0,2,1:T(8,128)S(1)} %get-tuple-element.38), channel_id=1, source_target_pairs={{1,0},{2,1},{3,2},{4,3},{5,4},{6,5},{7,6},{9,8},{10,9},{11,10},{12... | collective-permute-start | bytes 4718600 | tf_op jit(solution)/shard_map/ppermute | solution.py:23
where the time goes:
time: 227 us; the launch traced here: 226 us
  blocking collectives  88.7 us (39%)
  starting transfers between devices  47.1 us (21%)
  waiting for transfers between devices  44.7 us (20%)
  other arithmetic  35.2 us (16%)
  local copies, waits for them, and re-layouts  8.26 us (4%)
    psum x3, blocking collectives, pair_totals(): lax.psum((local_sum(residual, precond), local_sum(image, precond)), 'space')  88.7 us
    ppermute x6, starting transfers between devices, with_halo(): lax.ppermute(tail, axis, [(i, (i + 1) % count) for i in range(ends)])  35.2 us
    ppermute x2, waiting for transfers between devices, from_behind(): lax.ppermute(x, axis, [(i, (i + by) % devices) for i in range(devices)])  25.2 us
    reduce_sum x3, other arithmetic, local_sum(): return jnp.sum(left * right, axis=(1, 2, 3))  16.7 us
    ppermute x6, waiting for transfers between devices, with_halo(): lax.ppermute(head, axis, [((i + 1) % count, i) for i in range(ends)])  12.9 us
    div x3, other arithmetic, shards(): precond = residual / diag  8.38 us
    ppermute x6, starting transfers between devices, with_halo(): lax.ppermute(head, axis, [((i + 1) % count, i) for i in range(ends)])  8.06 us
    ppermute x6, waiting for transfers between devices, with_halo(): lax.ppermute(tail, axis, [(i, (i + 1) % count) for i in range(ends)])  6.6 us
  transfers between devices with their start and end apart: 14, of which 11 were waited for; matrix products, arithmetic and copies ran while one was open for 1% of the time, Pallas kernels for 0%

commit v1 on v0

v1 whole, which is shorter than its diff:
```python
import functools
import jax
import jax.numpy as jnp
from jax import lax
from jax.experimental import pallas as pl
from jax.experimental.pallas import tpu as pltpu
from jax.sharding import PartitionSpec as P

PARTNERS = 3
MASS = 0.5
LEFT = 4
RIGHT = 5
MOMENTS = 6
MESH = pl.DeviceIdType.MESH


def hops_of(reach, slab):
    found = []
    done = 0
    while done < reach:
        take = min(slab, reach - done)
        found.append((done, take))
        done += take
    return found


def ring_barrier(n_mode, n_space):
    mine = lax.axis_index("mode")
    place = lax.axis_index("space")
    barrier = pltpu.get_barrier_semaphore()
    for by in (1, n_space - 1):
        pl.semaphore_signal(barrier, inc=1, device_id=(mine, lax.rem(place + by, n_space)), device_id_type=MESH)
    for by in (1, 2, n_mode - 2, n_mode - 1):
        pl.semaphore_signal(barrier, inc=1, device_id=(lax.rem(mine + by, n_mode), place), device_id_type=MESH)
    pl.semaphore_wait(barrier, 6)


def gather_kernel(n_mode, n_space, slab, modes_ref, ids_ref, ext_ref, idx_ref, own_sem, ms, mr, zs, zr):
    mine = lax.axis_index("mode")
    place = lax.axis_index("space")
    right_hops = hops_of(LEFT, slab)
    left_hops = hops_of(RIGHT, slab)
    ring_barrier(n_mode, n_space)

    def z_copy(group, toward_right, hop):
        done, take = (right_hops if toward_right else left_hops)[hop]
        if toward_right:
            dst = LEFT - done - take
            src = dst + slab
            target = place + 1
        else:
            dst = LEFT + slab + done
            src = dst - slab
            target = place - 1
        if group == PARTNERS:
            src_ref, dst_ref = idx_ref.at[pl.ds(src, take)], idx_ref.at[pl.ds(dst, take)]
            if hop == 0:
                src_ref = ids_ref.at[pl.ds(src - LEFT, take)]
        else:
            src_ref, dst_ref = ext_ref.at[group, :, pl.ds(src, take)], ext_ref.at[group, :, pl.ds(dst, take)]
            if group == 0 and hop == 0:
                src_ref = modes_ref.at[:, pl.ds(src - LEFT, take)]
        side = 0 if toward_right else 1
        return pltpu.make_async_remote_copy(
            src_ref=src_ref,
            dst_ref=dst_ref,
            send_sem=zs.at[group, side, hop],
            recv_sem=zr.at[group, side, hop],
            device_id=(mine, jnp.clip(target, 0, n_space - 1)),
            device_id_type=MESH,
        )

    def sends(toward_right, hop):
        if toward_right:
            return jnp.logical_and(place < n_space - 1, place >= hop)
        return jnp.logical_and(place > 0, place + hop <= n_space - 1)

    def receives(toward_right, hop):
        if toward_right:
            return place >= hop + 1
        return place + hop + 1 <= n_space - 1

    def block_copy(step):
        return pltpu.make_async_remote_copy(
            src_ref=modes_ref,
            dst_ref=ext_ref.at[step, :, pl.ds(LEFT, slab)],
            send_sem=ms.at[step],
            recv_sem=mr.at[step],
            device_id=(lax.rem(mine + step, n_mode), place),
            device_id_type=MESH,
        )

    def each(group, hop, act):
        for toward_right, hops in ((True, right_hops), (False, left_hops)):
            if hop < len(hops):
                act(group, toward_right, hop)

    def start(group, toward_right, hop):
        @pl.when(sends(toward_right, hop))
        def _():
            z_copy(group, toward_right, hop).start()

    def arrive(group, toward_right, hop):
        @pl.when(receives(toward_right, hop))
        def _():
            z_copy(group, toward_right, hop).wait_recv()

    def leave(group, toward_right, hop):
        @pl.when(sends(toward_right, hop))
        def _():
            z_copy(group, toward_right, hop).wait_send()

    depth = max(len(right_hops), len(left_hops))
    own = pltpu.make_async_copy(modes_ref, ext_ref.at[0, :, pl.ds(LEFT, slab)], own_sem.at[0])
    own_ids = pltpu.make_async_copy(ids_ref, idx_ref.at[pl.ds(LEFT, slab)], own_sem.at[1])
    for group in (0, PARTNERS):
        each(group, 0, start)
    for step in range(1, PARTNERS):
        block_copy(step).start()
    own.start()
    own_ids.start()
    for group in [0, PARTNERS] + list(range(1, PARTNERS)):
        if 0 < group < PARTNERS:
            block_copy(group).wait_recv()
            each(group, 0, start)
        for hop in range(depth):
            each(group, hop, arrive)
            if hop + 1 < depth:
                each(group, hop + 1, start)
    own.wait()
    own_ids.wait()
    for step in range(1, PARTNERS):
        block_copy(step).wait_send()
    for group in range(PARTNERS + 1):
        for hop in range(depth):
            each(group, hop, leave)


def gather(n_mode, n_space, modes, ids):
    count, slab, ny, nz = modes.shape
    wide = LEFT + slab + RIGHT
    depth = max(len(hops_of(LEFT, slab)), len(hops_of(RIGHT, slab)))
    return pl.pallas_call(
        functools.partial(gather_kernel, n_mode, n_space, slab),
        out_shape=(
            jax.ShapeDtypeStruct((PARTNERS, count, wide, ny, nz), modes.dtype),
            jax.ShapeDtypeStruct((wide, ny, nz), ids.dtype),
        ),
        in_specs=[pl.BlockSpec(memory_space=pl.ANY)] * 2,
        out_specs=(pl.BlockSpec(memory_space=pl.ANY),) * 2,
        scratch_shapes=[
            pltpu.SemaphoreType.DMA((2,)),
            pltpu.SemaphoreType.DMA((PARTNERS,)),
            pltpu.SemaphoreType.DMA((PARTNERS,)),
            pltpu.SemaphoreType.DMA((PARTNERS + 1, 2, depth)),
            pltpu.SemaphoreType.DMA((PARTNERS + 1, 2, depth)),
        ],
        compiler_params=pltpu.CompilerParams(collective_id=0, has_side_effects=True),
    )(modes, ids)


def shifts(v):
    rows, lanes = v.shape
    return (
        pltpu.roll(v, 1, 0),
        pltpu.roll(v, rows - 1, 0),
        pltpu.roll(v, 1, 1),
        pltpu.roll(v, lanes - 1, 1),
    )


def edge_masks(shape):
    row = lax.broadcasted_iota(jnp.int32, shape, 0)
    lane = lax.broadcasted_iota(jnp.int32, shape, 1)
    return (row > 0, row < shape[0] - 1, lane > 0, lane < shape[1] - 1)


def plane_sum(v, masks):
    total = None
    for moved, keep in zip(shifts(v), masks):
        part = jnp.where(keep, moved, 0.0)
        total = part if total is None else total + part
    return total


def compute_kernel(
    slab, layers,
    plan_ref, stiff_ref, cubic_ref, place_ref, ext_ref, ids_ref,
    basis_ref, mom_ref,
    lap_own, lap_any, coeff, g_ref, dinv, diag_own, scaled, faces,
):
    s = pl.program_id(0)
    count = ext_ref.shape[1]
    shape = ext_ref.shape[-2:]
    wide = LEFT + slab + RIGHT
    base = place_ref[0] * slab - LEFT

    def valid(i):
        at = base + i
        return jnp.logical_and(at >= 0, at < layers)

    @pl.when(s == 0)
    def _():
        masks = edge_masks(shape)
        regions = stiff_ref.shape[0]
        for i in range(1, wide - 1):
            ids = jnp.where(valid(i), ids_ref[i].astype(jnp.float32), 0.0)
            c = jnp.zeros(shape, jnp.float32)
            g = jnp.zeros(shape, jnp.float32)
            for k in range(regions):
                hit = ids == float(k + 1)
                c = jnp.where(hit, stiff_ref[k], c)
                g = jnp.where(hit, cubic_ref[k], g)
            coeff[i - 1] = c
            g_ref[i - 1] = g
        for i in range(2, wide - 2):
            c = coeff[i - 1]
            near = [coeff[i - 2], coeff[i]]
            near += [jnp.where(keep, moved, 0.0) for moved, keep in zip(shifts(c), masks)]
            weights = [0.5 * (c + other) for other in near]
            diag = MASS + weights[0] + weights[1] + weights[2] + weights[3] + weights[4] + weights[5]
            inverse = jnp.where(valid(i), 1.0 / diag, 0.0)
            dinv[i - 2] = inverse
            inside = [weights[0], weights[1]] + [jnp.where(keep, w, 0.0) for w, keep in zip(weights[2:], masks)]
            if 3 <= i < wide - 3:
                for k in range(6):
                    scaled[i - 3, k] = inside[k] * inverse
            if LEFT <= i < LEFT + slab:
                diag_own[i - LEFT] = diag
                faces[i - LEFT, 0] = inside[1]
                faces[i - LEFT, 1] = inside[3]
                faces[i - LEFT, 2] = inside[5]

    def lap_step(j, carry):
        masks = edge_masks(shape)
        below = jnp.where(valid(0), ext_ref[0, j, 0].astype(jnp.float32), 0.0)
        here = jnp.where(valid(1), ext_ref[0, j, 1].astype(jnp.float32), 0.0)
        for i in range(1, wide - 1):
            above = jnp.where(valid(i + 1), ext_ref[0, j, i + 1].astype(jnp.float32), 0.0)
            out = 6.0 * here - (below + above + plane_sum(here, masks))
            lap_any[j, i - 1] = out

            @pl.when(s == 0)
            def _():
                lap_own[j, i - 1] = out * g_ref[i - 1]

            below, here = here, above
        return carry

    lax.fori_loop(0, count, lap_step, 0)

    def apply(v, i):
        below, here, above = v[i - 1], v[i], v[i + 1]
        up, down, west, east = shifts(here)
        w = [scaled[i - 3, k] for k in range(6)]
        return w[0] * below + w[1] * above + w[2] * up + w[3] * down + w[4] * west + w[5] * east

    def field_step(a, carry):
        masks = edge_masks(shape)
        j = plan_ref[a, s]
        prod, v0, v1, v2 = {}, {}, {}, {}
        sums = [None] * MOMENTS

        def add(k, value):
            sums[k] = value if sums[k] is None else sums[k] + value

        def own(i):
            return LEFT <= i < LEFT + slab

        for i in range(1, wide + 5):
            if i < wide - 1:
                prod[i] = lap_own[a, i - 1] * lap_any[j, i - 1]
            e = i - 1
            if 2 <= e < wide - 2:
                rhs = prod[e - 1] + prod[e + 1] + plane_sum(prod[e], masks) - 6.0 * prod[e]
                v0[e] = rhs * dinv[e - 2]
                if own(e):
                    basis_ref[0, a, e - LEFT] = v0[e]
                    add(0, rhs * v0[e])
            e = i - 2
            if 3 <= e < wide - 3:
                v1[e] = apply(v0, e)
                if own(e):
                    basis_ref[1, a, e - LEFT] = v1[e]
                    heavy = diag_own[e - LEFT] * v1[e]
                    add(1, heavy * v0[e])
                    add(2, heavy * v1[e])
            e = i - 3
            if LEFT <= e < wide - 4:
                v2[e] = apply(v1, e)
                if own(e):
                    basis_ref[2, a, e - LEFT] = v2[e]
                    heavy = diag_own[e - LEFT] * v2[e]
                    add(3, heavy * v1[e])
                    add(4, heavy * v2[e])
            e = i - 4
            if own(e):
                here = v2[e]
                up, down, west, east = shifts(here)
                flow = faces[e - LEFT, 0] * v2[e + 1] + faces[e - LEFT, 1] * down + faces[e - LEFT, 2] * east
                add(5, 2.0 * (flow * here))
        for k in range(MOMENTS):
            mom_ref[0, a, k] = jnp.sum(sums[k], axis=0)
        return carry

    lax.fori_loop(0, count, field_step, 0)


def compute(n_space, plan, stiffness, nonlinear, place, ext, ids, slab):
    _, count, wide, ny, nz = ext.shape
    plane = (ny, nz)
    smem = pl.BlockSpec(memory_space=pltpu.SMEM)
    return pl.pallas_call(
        functools.partial(compute_kernel, slab, n_space * slab),
        grid=(PARTNERS,),
        out_shape=(
            jax.ShapeDtypeStruct((PARTNERS, PARTNERS * count, slab, ny, nz), jnp.float32),
            jax.ShapeDtypeStruct((PARTNERS, count, MOMENTS, nz), jnp.float32),
        ),
        in_specs=[
            smem, smem, smem, smem,
            pl.BlockSpec((1, count, wide, ny, nz), lambda s: (s, 0, 0, 0, 0)),
            pl.BlockSpec((wide, ny, nz), lambda s: (0, 0, 0)),
        ],
        out_specs=(
            pl.BlockSpec((PARTNERS, count, slab, ny, nz), lambda s: (0, s, 0, 0, 0)),
            pl.BlockSpec((1, count, MOMENTS, nz), lambda s: (s, 0, 0, 0)),
        ),
        scratch_shapes=[
            pltpu.VMEM((count, wide - 2) + plane, jnp.float32),
            pltpu.VMEM((count, wide - 2) + plane, jnp.float32),
            pltpu.VMEM((wide - 2,) + plane, jnp.float32),
            pltpu.VMEM((wide - 2,) + plane, jnp.float32),
            pltpu.VMEM((wide - 4,) + plane, jnp.float32),
            pltpu.VMEM((slab,) + plane, jnp.float32),
            pltpu.VMEM((wide - 6, 6) + plane, jnp.float32),
            pltpu.VMEM((slab, 3) + plane, jnp.float32),
        ],
        compiler_params=pltpu.CompilerParams(vmem_limit_bytes=48 * 1024 * 1024),
    )(plan, stiffness, nonlinear, place, ext, ids)


def coefficients(m):
    zero = jnp.zeros_like(m[0])
    one = jnp.ones_like(m[0])

    def form(left, right, at):
        total = zero
        for i in range(3):
            for j in range(3):
                if left[i] is not None and right[j] is not None:
                    total = total + left[i] * right[j] * m[i + j + at]
        return total

    z = [one, None, None]
    p = [one, None, None]
    x = [zero, zero, zero]
    rz = m[0]
    for step in range(3):
        alpha = rz / (form(p, p, 0) - form(p, p, 1))
        x = [x[i] if p[i] is None else x[i] + alpha * p[i] for i in range(3)]
        if step == 2:
            break
        old = z
        z = []
        for i in range(3):
            change = zero if p[i] is None else p[i]
            if i > 0 and p[i - 1] is not None:
                change = change - p[i - 1]
            if i > step + 1:
                z.append(None)
            else:
                z.append((zero if old[i] is None else old[i]) - alpha * change)
        new = form(z, z, 0)
        ratio = new / rz
        p = [None if z[i] is None else z[i] + (ratio * p[i] if p[i] is not None else 0.0) for i in range(3)]
        rz = new
    return x


def reduce_kernel(n_space, mom_ref, out_ref, slots, ss, rs):
    mine = lax.axis_index("mode")
    place = lax.axis_index("space")
    barrier = pltpu.get_barrier_semaphore()
    for by in range(1, n_space):
        pl.semaphore_signal(barrier, inc=1, device_id=(mine, lax.rem(place + by, n_space)), device_id_type=MESH)
    pl.semaphore_wait(barrier, n_space - 1)
    copies = []
    for by in range(1, n_space):
        copy = pltpu.make_async_remote_copy(
            src_ref=mom_ref,
            dst_ref=slots.at[by],
            send_sem=ss.at[by],
            recv_sem=rs.at[by],
            device_id=(mine, lax.rem(place + by, n_space)),
            device_id_type=MESH,
        )
        copy.start()
        copies.append(copy)
    total = mom_ref[...]
    for by in range(1, n_space):
        copies[by - 1].wait_recv()
        total = total + slots[by]
    m = [total[k : k + 1] for k in range(MOMENTS)]
    found = coefficients(m)
    out_ref[...] = jnp.concatenate(found + [jnp.zeros_like(total[: total.shape[0] - 3])], 0)
    for copy in copies:
        copy.wait_send()


def reduce_moments(n_space, moments):
    return pl.pallas_call(
        functools.partial(reduce_kernel, n_space),
        out_shape=jax.ShapeDtypeStruct(moments.shape, jnp.float32),
        in_specs=[pl.BlockSpec(memory_space=pltpu.VMEM)],
        out_specs=pl.BlockSpec(memory_space=pltpu.VMEM),
        scratch_shapes=[
            pltpu.VMEM((n_space,) + moments.shape, jnp.float32),
            pltpu.SemaphoreType.DMA((n_space,)),
            pltpu.SemaphoreType.DMA((n_space,)),
        ],
        compiler_params=pltpu.CompilerParams(collective_id=1, has_side_effects=True),
    )(moments)


def shards(n_mode, n_space, modes, regions, stiffness, nonlinear, plan):
    count, slab, ny, nz = modes.shape
    place = lax.axis_index("space").astype(jnp.int32)[None]
    ids = (regions + 1).astype(jnp.bfloat16)
    ext, idx = gather(n_mode, n_space, modes, ids)
    basis, moments = compute(n_space, plan, stiffness, nonlinear, place, ext, idx, slab)
    fields = PARTNERS * count
    sums = jnp.sum(moments, -1).reshape(fields, MOMENTS).T
    sums = jnp.pad(sums, ((0, 8 - MOMENTS), (0, 128 - fields)))
    found = reduce_moments(n_space, sums)[:3, :fields, None, None, None]
    x = found[0] * basis[0] + found[1] * basis[1] + found[2] * basis[2]
    return jnp.swapaxes(x.reshape((PARTNERS, count, slab, ny, nz)), 0, 1)


def solution(mesh):
    return jax.shard_map(
        functools.partial(shards, mesh.shape["mode"], mesh.shape["space"]),
        mesh=mesh,
        in_specs=(
            P("mode", "space", None, None),
            P("space", None, None),
            P(),
            P(),
            P("mode", None),
        ),
        out_specs=P("mode", None, "space", None, None),
        check_vma=False,
    )
```

time: 227 us -> 153 us (0.67)
  Pallas kernels: 0 us -> 139 us
  blocking collectives: 88.7 us -> 0 us
  starting transfers between devices: 47.1 us -> 0 us
  waiting for transfers between devices: 44.7 us -> 0 us
  other arithmetic: 35.2 us -> 3.95 us
    pallas_call x0 -> x3, Pallas kernels: none -> 139 us  [the longest x1 68.9 us: gather(): pl.pallas_call(functools.partial(gather_kernel, n_mode, n_space, slab), o...]
    psum x3 -> x0, blocking collectives: 88.7 us -> none  [pair_totals(): lax.psum((local_sum(residual, precond), local_sum(image, precond)), 'space')]
    ppermute x14 -> x0, starting transfers between devices: 47.1 us -> none  [the longest x6 35.2 us: with_halo(): lax.ppermute(tail, axis, [(i, (i + 1) % count) for i in range(ends)])]
    ppermute x14 -> x0, waiting for transfers between devices: 44.7 us -> none  [the longest x2 25.2 us: from_behind(): lax.ppermute(x, axis, [(i, (i + by) % devices) for i in range(devices)])]
    reduce_sum x4 -> x1, other arithmetic: 17 us -> 0.12 us  [shards(): sums = jnp.sum(moments, -1).reshape(fields, MOMENTS).T]
    div x6 -> x0, other arithmetic: 10.3 us -> none  [the longest x3 8.38 us: shards(): precond = residual / diag]
    add x4 -> x0, other arithmetic: 5.05 us -> none  [the longest x1 4.1 us: shards(): solution = solution + expand(alpha) * direction]
    slice x9 -> x2, local copies, waits for them, and re-layouts: 1.15 us -> 5.55 us  [shards(): x = found[0] * basis[0] + found[1] * basis[1] + found[2] * basis[2]]
  transfers between devices with their start and end apart: 14 -> 0, of which waited for: 11 -> 0; matrix products, arithmetic and copies ran while one was open for 1% -> 0% of each run, Pallas kernels for 0% -> 0%
where the time goes in v1:
time: 153 us
  Pallas kernels  139 us (91%)
  local copies, waits for them, and re-layouts  9.72 us (6%)
  other arithmetic  3.95 us (3%)
    pallas_call x1, Pallas kernels, gather(): pl.pallas_call(functools.partial(gather_kernel, n_mode, n_space, slab), o...  68.9 us
    pallas_call x1, Pallas kernels, compute(): pl.pallas_call(functools.partial(compute_kernel, slab, n_space * slab), g...  60.7 us
    pallas_call x1, Pallas kernels, reduce_moments(): pl.pallas_call(functools.partial(reduce_kernel, n_space), out_shape=jax.S...  9.8 us
    slice x2, local copies, waits for them, and re-layouts, shards(): x = found[0] * basis[0] + found[1] * basis[1] + found[2] * basis[2]  5.55 us

profile of v1, /device:TPU:0, one launch (start us, length us, event | category | flops | bytes accessed | tf_op | source)
XLA Modules:
  0.0 153.1 jit_solution(7954320721694414351)
XLA Ops:
  0.0 0.8 copy.13.plan_ref
  0.8 1.5 add_convert_fusion.ids_ref
  2.2 68.9 %shard_map.55 = (bf16[3,16,11,64,128]{4,3,2,1,0:T(8,128)(2,1)}, bf16[11,64,128]{2,1,0:T(8,128)(2,1)}) custom-call(bf16[16,2,64,128]{3,2,1,0:T(8,128)(2,1)} %modes_ref.1, bf16[2,64,128]{2,1,0:T(8,128)(2,1)} %add_convert_fusion.ids_ref), custom_call_target="tpu_custom_call" | custom-call | tf_op jit(solution)/shard_map/pallas_call | solution.py:143
  71.2 0.0 copy-start
  71.2 0.9 copy-done
  72.1 0.0 copy-start.1
  72.1 0.7 copy-done.1
  72.7 0.0 copy-start.2
  72.7 0.7 copy-done.2
  73.4 60.7 %shard_map.56 = (f32[3,48,2,64,128]{4,3,2,1,0:T(8,128)}, f32[3,16,6,128]{3,2,1,0:T(8,128)S(1)}) custom-call(s32[16,3]{1,0:T(8,128)S(1)} %copy.13.plan_ref, f32[8]{0:T(128)S(1)} %copy-done.1, f32[8]{0:T(128)S(1)} %copy-done.2, s32[1]{0:T(128)} %bitcast.place_ref, bf16[3,16,11,64,128]{4,3,2,1,0:T(8,128)(2,1)} %get-tuple-element.9.ext_ref, ...), custom_call_target="tpu_custom_call" | custom-call | tf_op jit(solution)/shard_map/pallas_call | solution.py:313
  134.1 0.1 reduce_sum.9
  134.2 0.1 copy.21
  134.3 0.6 pad.4.mom_ref
  134.9 9.8 %shard_map.57 = f32[8,128]{1,0:T(8,128)} custom-call(f32[8,128]{1,0:T(8,128)} %pad.4.mom_ref), custom_call_target="tpu_custom_call" | custom-call | tf_op jit(solution)/shard_map/pallas_call | solution.py:412
  144.7 0.8 slice_reduce_fusion.2
  145.5 0.1 mul.33
  145.6 0.1 mul.39
  145.7 0.1 mul.36
  145.7 0.1 copy.17
  145.8 0.1 copy.19
  145.9 0.1 copy.15
  146.0 4.7 %fusion.3 = (f32[1,48,2,64,128]{4,3,2,1,0:T(8,128)S(1)}, f32[1,48,2,64,128]{4,3,2,1,0:T(8,128)S(1)}, f32[1,48,2,64,128]{4,3,2,1,0:T(8,128)S(1)}) fusion(f32[3,48,2,64,128]{4,3,2,1,0:T(8,128)} %get-tuple-element.12), kind=kLoop, calls=%fused_computation.10 | loop fusion | bytes 18874368 | tf_op jit(solution)/shard_map/slice | solution.py:436
  150.7 2.4 %fusion.1 = f32[16,3,2,64,128]{4,3,2,1,0:T(8,128)} fusion(f32[3,16,2,64,128]{4,3,2,1,0:T(8,128)S(1)} %bitcast.9, f32[3,16,2,64,128]{4,3,2,1,0:T(8,128)S(1)} %bitcast.10, f32[3,16,2,64,128]{4,3,2,1,0:T(8,128)S(1)} %bitcast.8, f32[3,16]{0,1:T(8,128)S(1)} %copy.19, f32[3,16]{0,1:T(8,128)S(1)} %copy.17, f32[3,16]{0,1:T(8,128)S(1)} %copy.15), kind=kLoop, calls=%fused_computation.2 | loop fusion | flops 3932160 | bytes 12583488 | tf_op jit(solution)/shard_map/transpose | solution.py:437
Async XLA Ops:
  71.2 0.9 copy-start
  72.1 0.7 copy-start.1
  72.7 0.7 copy-start.2

commit v2 on v1

v2 whole, which is shorter than its diff:
```python
import functools
import jax
import jax.numpy as jnp
from jax import lax
from jax.experimental import pallas as pl
from jax.experimental.pallas import tpu as pltpu
from jax.sharding import PartitionSpec as P

PARTNERS = 3
MASS = 0.5
LEFT = 4
RIGHT = 5
MOMENTS = 6
MESH = pl.DeviceIdType.MESH


def hops_of(reach, slab):
    found = []
    done = 0
    while done < reach:
        take = min(slab, reach - done)
        found.append((done, take))
        done += take
    return found


def shifts(v):
    rows, lanes = v.shape
    return (
        pltpu.roll(v, 1, 0),
        pltpu.roll(v, rows - 1, 0),
        pltpu.roll(v, 1, 1),
        pltpu.roll(v, lanes - 1, 1),
    )


def edge_masks(shape):
    row = lax.broadcasted_iota(jnp.int32, shape, 0)
    lane = lax.broadcasted_iota(jnp.int32, shape, 1)
    return (row > 0, row < shape[0] - 1, lane > 0, lane < shape[1] - 1)


def stencil_matrix(size, middle):
    row = lax.broadcasted_iota(jnp.int32, (size, size), 0)
    column = lax.broadcasted_iota(jnp.int32, (size, size), 1)
    beside = jnp.logical_or(row == column + 1, column == row + 1)
    return jnp.where(row == column, middle, jnp.where(beside, -1.0, 0.0)).astype(jnp.bfloat16)


def dot(left, right):
    return jnp.dot(left, right, preferred_element_type=jnp.float32)


def kernel(
    n_mode, n_space, count, slab,
    plan_ref, stiff_ref, cubic_ref, modes_ref, ids_ref,
    out_ref,
    ext_ref, idx_ref, lap_own, lap_any, coeff, g_ref, dinv, diag_own, scaled, faces,
    lanes_mat, rows_mat, basis_ref, mom_ref, sums_ref, slots, coef_ref,
    own_sem, ms, mr, zs, zr, ss, rs,
):
    mine = lax.axis_index("mode")
    place = lax.axis_index("space")
    shape = ext_ref.shape[-2:]
    wide = LEFT + slab + RIGHT
    layers = n_space * slab
    base = place * slab - LEFT
    right_hops = hops_of(LEFT, slab)
    left_hops = hops_of(RIGHT, slab)

    barrier = pltpu.get_barrier_semaphore()
    for by in range(1, n_space):
        pl.semaphore_signal(barrier, inc=1, device_id=(mine, lax.rem(place + by, n_space)), device_id_type=MESH)
    for by in (1, 2, n_mode - 2, n_mode - 1):
        pl.semaphore_signal(barrier, inc=1, device_id=(lax.rem(mine + by, n_mode), place), device_id_type=MESH)
    pl.semaphore_wait(barrier, n_space - 1 + 4)

    def z_copy(group, toward_right, hop):
        done, take = (right_hops if toward_right else left_hops)[hop]
        if toward_right:
            dst = LEFT - done - take
            src = dst + slab
            target = place + 1
        else:
            dst = LEFT + slab + done
            src = dst - slab
            target = place - 1
        if group == PARTNERS:
            src_ref, dst_ref = idx_ref.at[pl.ds(src, take)], idx_ref.at[pl.ds(dst, take)]
            if hop == 0:
                src_ref = ids_ref.at[pl.ds(src - LEFT, take)]
        else:
            src_ref, dst_ref = ext_ref.at[group, :, pl.ds(src, take)], ext_ref.at[group, :, pl.ds(dst, take)]
            if group == 0 and hop == 0:
                src_ref = modes_ref.at[:, pl.ds(src - LEFT, take)]
        side = 0 if toward_right else 1
        return pltpu.make_async_remote_copy(
            src_ref=src_ref,
            dst_ref=dst_ref,
            send_sem=zs.at[group, side, hop],
            recv_sem=zr.at[group, side, hop],
            device_id=(mine, jnp.clip(target, 0, n_space - 1)),
            device_id_type=MESH,
        )

    def sends(toward_right, hop):
        if toward_right:
            return jnp.logical_and(place < n_space - 1, place >= hop)
        return jnp.logical_and(place > 0, place + hop <= n_space - 1)

    def receives(toward_right, hop):
        if toward_right:
            return place >= hop + 1
        return place + hop + 1 <= n_space - 1

    def block_copy(step):
        return pltpu.make_async_remote_copy(
            src_ref=modes_ref,
            dst_ref=ext_ref.at[step, :, pl.ds(LEFT, slab)],
            send_sem=ms.at[step],
            recv_sem=mr.at[step],
            device_id=(lax.rem(mine + step, n_mode), place),
            device_id_type=MESH,
        )

    def each(group, hop, act):
        for toward_right, hops in ((True, right_hops), (False, left_hops)):
            if hop < len(hops):
                act(group, toward_right, hop)

    def start(group, toward_right, hop):
        @pl.when(sends(toward_right, hop))
        def _():
            z_copy(group, toward_right, hop).start()

    def arrive(group, toward_right, hop):
        @pl.when(receives(toward_right, hop))
        def _():
            z_copy(group, toward_right, hop).wait_recv()

    def leave(group, toward_right, hop):
        @pl.when(sends(toward_right, hop))
        def _():
            z_copy(group, toward_right, hop).wait_send()

    depth = max(len(right_hops), len(left_hops))

    def advance(group, hop):
        each(group, hop, arrive)
        if hop + 1 < depth:
            each(group, hop + 1, start)

    def open_block(group):
        block_copy(group).wait_recv()
        each(group, 0, start)

    def set_up():
        masks = edge_masks(shape)
        regions = stiff_ref.shape[0]
        for i in range(1, wide - 1):
            ids = idx_ref[i].astype(jnp.float32)
            c = jnp.zeros(shape, jnp.float32)
            g = jnp.zeros(shape, jnp.float32)
            for k in range(regions):
                hit = ids == float(k + 1)
                c = jnp.where(hit, stiff_ref[k], c)
                g = jnp.where(hit, cubic_ref[k], g)
            coeff[i - 1] = c
            g_ref[i - 1] = g
        for i in range(2, wide - 2):
            c = coeff[i - 1]
            near = [coeff[i - 2], coeff[i]]
            near += [jnp.where(keep, moved, 0.0) for moved, keep in zip(shifts(c), masks)]
            weights = [0.5 * (c + other) for other in near]
            diag = MASS + weights[0] + weights[1] + weights[2] + weights[3] + weights[4] + weights[5]
            inside_grid = jnp.logical_and(base + i >= 0, base + i < layers).astype(jnp.float32)
            inverse = inside_grid / diag
            dinv[i - 2] = inverse
            inside = [weights[0], weights[1]] + [jnp.where(keep, w, 0.0) for w, keep in zip(weights[2:], masks)]
            if 3 <= i < wide - 3:
                for k in range(6):
                    scaled[i - 3, k] = inside[k] * inverse
            if LEFT <= i < LEFT + slab:
                diag_own[i - LEFT] = diag
                faces[i - LEFT, 0] = inside[1]
                faces[i - LEFT, 1] = inside[3]
                faces[i - LEFT, 2] = inside[5]

    def lap_loop(group):
        def lap_step(j, carry):
            across = lanes_mat[: shape[1]]
            along = rows_mat[:, : shape[0]]
            raw = [ext_ref[group, j, i] for i in range(wide)]
            plain = [v.astype(jnp.float32) for v in raw]
            for i in range(1, wide - 1):
                out = dot(raw[i], across) + dot(along, raw[i]) - (plain[i - 1] + plain[i + 1])
                lap_any[j, i - 1] = out
                if group == 0:
                    lap_own[j, i - 1] = out * g_ref[i - 1]
            return carry

        lax.fori_loop(0, count, lap_step, 0)

    def apply(v, i):
        below, here, above = v[i - 1], v[i], v[i + 1]
        up, down, west, east = shifts(here)
        w = [scaled[i - 3, k] for k in range(6)]
        return w[0] * below + w[1] * above + w[2] * up + w[3] * down + w[4] * west + w[5] * east

    def field_loop(s, first, last):
        def field_step(a, carry):
            j = plan_ref[a, s]
            prod, v0, v1, v2 = {}, {}, {}, {}
            sums = [None] * MOMENTS

            def add(k, value):
                sums[k] = value if sums[k] is None else sums[k] + value

            def own(i):
                return LEFT <= i < LEFT + slab

            for i in range(1, wide + 5):
                if i < wide - 1:
                    prod[i] = lap_own[a, i - 1] * lap_any[j, i - 1]
                e = i - 1
                if 2 <= e < wide - 2:
                    high = prod[e].astype(jnp.bfloat16)
                    low = (prod[e] - high.astype(jnp.float32)).astype(jnp.bfloat16)
                    rhs = prod[e - 1] + prod[e + 1]
                    rhs = rhs - dot(jnp.concatenate([high, low], 1), lanes_mat[...])
                    rhs = rhs - dot(rows_mat[...], jnp.concatenate([high, low], 0))
                    v0[e] = rhs * dinv[e - 2]
                    if own(e):
                        basis_ref[0, s, a, e - LEFT] = v0[e]
                        add(0, rhs * v0[e])
                e = i - 2
                if 3 <= e < wide - 3:
                    v1[e] = apply(v0, e)
                    if own(e):
                        basis_ref[1, s, a, e - LEFT] = v1[e]
                        heavy = diag_own[e - LEFT] * v1[e]
                        add(1, heavy * v0[e])
                        add(2, heavy * v1[e])
                e = i - 3
                if LEFT <= e < wide - 4:
                    v2[e] = apply(v1, e)
                    if own(e):
                        basis_ref[2, s, a, e - LEFT] = v2[e]
                        heavy = diag_own[e - LEFT] * v2[e]
                        add(3, heavy * v1[e])
                        add(4, heavy * v2[e])
                e = i - 4
                if own(e):
                    here = v2[e]
                    up, down, west, east = shifts(here)
                    flow = faces[e - LEFT, 0] * v2[e + 1] + faces[e - LEFT, 1] * down + faces[e - LEFT, 2] * east
                    add(5, 2.0 * (flow * here))
            for k in range(MOMENTS):
                mom_ref[k, pl.ds(s * count + a, 1), :] = jnp.sum(sums[k], axis=0, keepdims=True)
            return carry

        lax.fori_loop(first, last, field_step, 0)

    own = pltpu.make_async_copy(modes_ref, ext_ref.at[0, :, pl.ds(LEFT, slab)], own_sem.at[0])
    own_ids = pltpu.make_async_copy(ids_ref, idx_ref.at[pl.ds(LEFT, slab)], own_sem.at[1])
    for group in (0, PARTNERS):
        each(group, 0, start)
    for step in range(1, PARTNERS):
        block_copy(step).start()
    own.start()
    own_ids.start()
    for i in list(range(LEFT)) + list(range(LEFT + slab, wide)):
        @pl.when(base + i < 0 if i < LEFT else base + i >= layers)
        def _():
            idx_ref[i] = jnp.zeros(shape, idx_ref.dtype)

            def clear(j, carry):
                for group in range(PARTNERS):
                    ext_ref[group, j, i] = jnp.zeros(shape, ext_ref.dtype)
                return carry

            lax.fori_loop(0, count, clear, 0)
    lanes_mat[...] = jnp.concatenate([stencil_matrix(shape[1], 6.0)] * 2, 0)
    rows_mat[...] = jnp.concatenate([stencil_matrix(shape[0], 0.0)] * 2, 1)
    mom_ref[...] = jnp.zeros_like(mom_ref)
    own.wait()
    own_ids.wait()

    for hop in range(depth):
        advance(PARTNERS, hop)
        advance(0, hop)
        if hop == min(1, depth - 1):
            open_block(1)
    set_up()
    lap_loop(0)
    half = count // 2
    advance(1, 0)
    open_block(2)
    field_loop(0, 0, half)
    for hop in range(1, depth):
        advance(1, hop)
        advance(2, hop - 1)
        if hop == 1:
            field_loop(0, half, count)
    lap_loop(1)
    field_loop(1, 0, count)
    advance(2, depth - 1)
    lap_loop(2)
    field_loop(2, 0, count)

    ones = jnp.ones((8, shape[1]), jnp.float32)
    rows = []
    for k in range(MOMENTS):
        rows.append(
            lax.dot_general(
                ones, mom_ref[k], (((1,), (1,)), ((), ())),
                precision=lax.Precision.HIGHEST, preferred_element_type=jnp.float32,
            )[:1]
        )
    rows.append(jnp.zeros((8 - MOMENTS, mom_ref.shape[1]), jnp.float32))
    sums_ref[...] = jnp.concatenate(rows, 0)
    copies = []
    for by in range(1, n_space):
        copy = pltpu.make_async_remote_copy(
            src_ref=sums_ref,
            dst_ref=slots.at[by],
            send_sem=ss.at[by],
            recv_sem=rs.at[by],
            device_id=(mine, lax.rem(place + by, n_space)),
            device_id_type=MESH,
        )
        copy.start()
        copies.append(copy)
    total = sums_ref[...]
    for by in range(1, n_space):
        copies[by - 1].wait_recv()
        total = total + slots[by]
    found = coefficients([total[k : k + 1] for k in range(MOMENTS)])
    for k in range(3):
        coef_ref[k] = jnp.transpose(jnp.broadcast_to(found[k], coef_ref.shape[1:]))

    for s in range(PARTNERS):
        def combine(a, carry):
            c = [coef_ref[k, pl.ds(s * count + a, 1), :] for k in range(3)]
            for i in range(slab):
                out_ref[a, s, i] = (
                    c[0] * basis_ref[0, s, a, i] + c[1] * basis_ref[1, s, a, i] + c[2] * basis_ref[2, s, a, i]
                )
            return carry

        lax.fori_loop(0, count, combine, 0)

    for copy in copies:
        copy.wait_send()
    for step in range(1, PARTNERS):
        block_copy(step).wait_send()
    for group in range(PARTNERS + 1):
        for hop in range(depth):
            each(group, hop, leave)


def shards(n_mode, n_space, modes, regions, stiffness, nonlinear, plan):
    count, slab, ny, nz = modes.shape
    ids = (regions + 1).astype(jnp.bfloat16)
    wide = LEFT + slab + RIGHT
    depth = max(len(hops_of(LEFT, slab)), len(hops_of(RIGHT, slab)))
    padded = -(-PARTNERS * count // nz) * nz
    plane = (ny, nz)
    smem = pl.BlockSpec(memory_space=pltpu.SMEM)
    vmem = pl.BlockSpec(memory_space=pltpu.VMEM)
    return pl.pallas_call(
        functools.partial(kernel, n_mode, n_space, count, slab),
        out_shape=jax.ShapeDtypeStruct((count, PARTNERS, slab, ny, nz), jnp.float32),
        in_specs=[smem, smem, smem, vmem, vmem],
        out_specs=vmem,
        scratch_shapes=[
            pltpu.VMEM((PARTNERS, count, wide) + plane, modes.dtype),
            pltpu.VMEM((wide,) + plane, ids.dtype),
            pltpu.VMEM((count, wide - 2) + plane, jnp.float32),
            pltpu.VMEM((count, wide - 2) + plane, jnp.float32),
            pltpu.VMEM((wide - 2,) + plane, jnp.float32),
            pltpu.VMEM((wide - 2,) + plane, jnp.float32),
            pltpu.VMEM((wide - 4,) + plane, jnp.float32),
            pltpu.VMEM((slab,) + plane, jnp.float32),
            pltpu.VMEM((wide - 6, 6) + plane, jnp.float32),
            pltpu.VMEM((slab, 3) + plane, jnp.float32),
            pltpu.VMEM((2 * nz, nz), jnp.bfloat16),
            pltpu.VMEM((ny, 2 * ny), jnp.bfloat16),
            pltpu.VMEM((3, PARTNERS, count, slab) + plane, jnp.float32),
            pltpu.VMEM((MOMENTS, padded, nz), jnp.float32),
            pltpu.VMEM((8, padded), jnp.float32),
            pltpu.VMEM((n_space, 8, padded), jnp.float32),
            pltpu.VMEM((3, padded, padded), jnp.float32),
            pltpu.SemaphoreType.DMA((2,)),
            pltpu.SemaphoreType.DMA((PARTNERS,)),
            pltpu.SemaphoreType.DMA((PARTNERS,)),
            pltpu.SemaphoreType.DMA((PARTNERS + 1, 2, depth)),
            pltpu.SemaphoreType.DMA((PARTNERS + 1, 2, depth)),
            pltpu.SemaphoreType.DMA((n_space,)),
            pltpu.SemaphoreType.DMA((n_space,)),
        ],
        compiler_params=pltpu.CompilerParams(
            collective_id=0, has_side_effects=True, vmem_limit_bytes=52 * 1024 * 1024
        ),
    )(plan, stiffness, nonlinear, modes, ids)


def coefficients(m):
    zero = jnp.zeros_like(m[0])
    one = jnp.ones_like(m[0])

    def form(left, right, at):
        total = zero
        for i in range(3):
            for j in range(3):
                if left[i] is not None and right[j] is not None:
                    total = total + left[i] * right[j] * m[i + j + at]
        return total

    z = [one, None, None]
    p = [one, None, None]
    x = [zero, zero, zero]
    rz = m[0]
    for step in range(3):
        alpha = rz / (form(p, p, 0) - form(p, p, 1))
        x = [x[i] if p[i] is None else x[i] + alpha * p[i] for i in range(3)]
        if step == 2:
            break
        old = z
        z = []
        for i in range(3):
            change = zero if p[i] is None else p[i]
            if i > 0 and p[i - 1] is not None:
                change = change - p[i - 1]
            if i > step + 1:
                z.append(None)
            else:
                z.append((zero if old[i] is None else old[i]) - alpha * change)
        new = form(z, z, 0)
        ratio = new / rz
        p = [None if z[i] is None else z[i] + (ratio * p[i] if p[i] is not None else 0.0) for i in range(3)]
        rz = new
    return x


def solution(mesh):
    return jax.shard_map(
        functools.partial(shards, mesh.shape["mode"], mesh.shape["space"]),
        mesh=mesh,
        in_specs=(
            P("mode", "space", None, None),
            P("space", None, None),
            P(),
            P(),
            P("mode", None),
        ),
        out_specs=P("mode", None, "space", None, None),
        check_vma=False,
    )
```

time: 153 us -> 92.1 us (0.60)
  Pallas kernels: 139 us -> 83.9 us
  other arithmetic: 3.95 us -> 0.85 us
  local copies, waits for them, and re-layouts: 9.72 us -> 7.07 us
    pallas_call x3 -> x1, Pallas kernels: 139 us -> 83.9 us  [shards(): pl.pallas_call(functools.partial(kernel, n_mode, n_space, count, slab), o...]
    slice x2 -> x0, local copies, waits for them, and re-layouts: 5.55 us -> none  [shards(): x = found[0] * basis[0] + found[1] * basis[1] + found[2] * basis[2]]
    unnamed x7 -> x8, local copies, waits for them, and re-layouts: 2.98 us -> 7.07 us
    transpose x1 -> x0, other arithmetic: 2.37 us -> none  [shards(): return jnp.swapaxes(x.reshape((PARTNERS, count, slab, ny, nz)), 0, 1)]
where the time goes in v2:
time: 92.1 us; the launch traced here: 91.8 us
  Pallas kernels  83.9 us (91%)
  local copies, waits for them, and re-layouts  7.07 us (8%)
    pallas_call x1, Pallas kernels, shards(): pl.pallas_call(functools.partial(kernel, n_mode, n_space, count, slab), o...  83.9 us
    unnamed x8, local copies, waits for them, and re-layouts  7.07 us

profile of v2, /device:TPU:0, one launch (start us, length us, event | category | flops | bytes accessed | tf_op | source)
XLA Modules:
  0.0 91.8 jit_solution(1927572522948469735)
XLA Ops:
  0.0 0.8 copy.6.plan_ref
  0.8 0.8 add_convert_fusion.ids_ref
  1.6 0.0 copy-start
  1.6 1.0 %copy-done = bf16[16,2,64,128]{3,2,1,0:T(8,128)(2,1)S(1)} copy-done((bf16[16,2,64,128]{3,2,1,0:T(8,128)(2,1)S(1)}, bf16[16,2,64,128]{3,2,1,0:T(8,128)(2,1)}, u32[]{:S(2)}) %copy-start) | copy-done | bytes 524312
  2.7 0.0 copy-start.1
  2.7 0.7 copy-done.1
  3.3 0.0 copy-start.2
  3.3 0.7 copy-done.2
  4.0 83.9 %shard_map.55 = f32[16,3,2,64,128]{4,3,2,1,0:T(8,128)} custom-call(s32[16,3]{1,0:T(8,128)S(1)} %copy.6.plan_ref, f32[8]{0:T(128)S(1)} %copy-done.1, f32[8]{0:T(128)S(1)} %copy-done.2, bf16[16,2,64,128]{3,2,1,0:T(8,128)(2,1)S(1)} %copy-done, bf16[2,64,128]{2,1,0:T(8,128)(2,1)S(1)} %add_convert_fusion.ids_ref), custom_call_target="tpu_custom_call" | custom-call | tf_op jit(solution)/shard_map/pallas_call | solution.py:371
  87.9 4.0 %copy.8 = f32[16,3,2,64,128]{4,3,2,1,0:T(8,128)} copy(f32[16,3,2,64,128]{4,3,2,1,0:T(8,128)} %shard_map.55) | data formatting | bytes 6291456
Async XLA Ops:
  1.6 1.0 %copy-start = (bf16[16,2,64,128]{3,2,1,0:T(8,128)(2,1)S(1)}, bf16[16,2,64,128]{3,2,1,0:T(8,128)(2,1)}, u32[]{:S(2)}) copy-start(bf16[16,2,64,128]{3,2,1,0:T(8,128)(2,1)} %modes_ref.1) | copy-start | bytes 1572868
  2.7 0.7 copy-start.1
  3.3 0.7 copy-start.2

commit v3 on v2

--- a/solution.py
+++ b/solution.py
@@ -7,6 +7,8 @@
 from jax.sharding import PartitionSpec as P
 
 PARTNERS = 3
+SUBS = 2
+CHUNKS = 4
 MASS = 0.5
 LEFT = 4
 RIGHT = 5
@@ -75,7 +77,7 @@
         pl.semaphore_signal(barrier, inc=1, device_id=(lax.rem(mine + by, n_mode), place), device_id_type=MESH)
     pl.semaphore_wait(barrier, n_space - 1 + 4)
 
-    def z_copy(group, toward_right, hop):
+    def z_copy(group, toward_right, hop, sub):
         done, take = (right_hops if toward_right else left_hops)[hop]
         if toward_right:
             dst = LEFT - done - take
@@ -90,15 +92,16 @@
             if hop == 0:
                 src_ref = ids_ref.at[pl.ds(src - LEFT, take)]
         else:
-            src_ref, dst_ref = ext_ref.at[group, :, pl.ds(src, take)], ext_ref.at[group, :, pl.ds(dst, take)]
+            some = pl.ds(sub * part, part)
+            src_ref, dst_ref = ext_ref.at[group, some, pl.ds(src, take)], ext_ref.at[group, some, pl.ds(dst, take)]
             if group == 0 and hop == 0:
-                src_ref = modes_ref.at[:, pl.ds(src - LEFT, take)]
+                src_ref = modes_ref.at[some, pl.ds(src - LEFT, take)]
         side = 0 if toward_right else 1
         return pltpu.make_async_remote_copy(
             src_ref=src_ref,
             dst_ref=dst_ref,
-            send_sem=zs.at[group, side, hop],
-            recv_sem=zr.at[group, side, hop],
+            send_sem=zs.at[group, side, hop, sub],
+            recv_sem=zr.at[group, side, hop, sub],
             device_id=(mine, jnp.clip(target, 0, n_space - 1)),
             device_id_type=MESH,
         )
@@ -123,36 +126,41 @@
             device_id_type=MESH,
         )
 
-    def each(group, hop, act):
+    part = count // SUBS
+
+    def each(group, hop, sub, act):
         for toward_right, hops in ((True, right_hops), (False, left_hops)):
             if hop < len(hops):
-                act(group, toward_right, hop)
-
-    def start(group, toward_right, hop):
+                act(group, toward_right, hop, sub)
+
+    def start(group, toward_right, hop, sub):
         @pl.when(sends(toward_right, hop))
         def _():
-            z_copy(group, toward_right, hop).start()
-
-    def arrive(group, toward_right, hop):
+            z_copy(group, toward_right, hop, sub).start()
+
+    def arrive(group, toward_right, hop, sub):
         @pl.when(receives(toward_right, hop))
         def _():
-            z_copy(group, toward_right, hop).wait_recv()
-
-    def leave(group, toward_right, hop):
+            z_copy(group, toward_right, hop, sub).wait_recv()
+
+    def leave(group, toward_right, hop, sub):
         @pl.when(sends(toward_right, hop))
         def _():
-            z_copy(group, toward_right, hop).wait_send()
+            z_copy(group, toward_right, hop, sub).wait_send()
 
     depth = max(len(right_hops), len(left_hops))
 
-    def advance(group, hop):
-        each(group, hop, arrive)
+    def advance(group, hop, sub):
+        each(group, hop, sub, arrive)
         if hop + 1 < depth:
-            each(group, hop + 1, start)
+            each(group, hop + 1, sub, start)
 
     def open_block(group):
         block_copy(group).wait_recv()
-        each(group, 0, start)
+        if group + 1 < PARTNERS:
+            block_copy(group + 1).start()
+        for sub in range(SUBS):
+            each(group, 0, sub, start)
 
     def set_up():
         masks = edge_masks(shape)
@@ -186,13 +194,13 @@
                 faces[i - LEFT, 1] = inside[3]
                 faces[i - LEFT, 2] = inside[5]
 
-    def lap_loop(group):
+    def lap_loop(group, first, last):
         def lap_step(j, carry):
             across = lanes_mat[: shape[1]]
             along = rows_mat[:, : shape[0]]
-            raw = [ext_ref[group, j, i] for i in range(wide)]
-            plain = [v.astype(jnp.float32) for v in raw]
-            for i in range(1, wide - 1):
+            raw = {i: ext_ref[group, j, i] for i in range(first - 1, last + 1)}
+            plain = {i: raw[i].astype(jnp.float32) for i in raw}
+            for i in range(first, last):
                 out = dot(raw[i], across) + dot(along, raw[i]) - (plain[i - 1] + plain[i + 1])
                 lap_any[j, i - 1] = out
                 if group == 0:
@@ -263,10 +271,10 @@
 
     own = pltpu.make_async_copy(modes_ref, ext_ref.at[0, :, pl.ds(LEFT, slab)], own_sem.at[0])
     own_ids = pltpu.make_async_copy(ids_ref, idx_ref.at[pl.ds(LEFT, slab)], own_sem.at[1])
-    for group in (0, PARTNERS):
-        each(group, 0, start)
-    for step in range(1, PARTNERS):
-        block_copy(step).start()
+    each(PARTNERS, 0, 0, start)
+    for sub in range(SUBS):
+        each(0, 0, sub, start)
+    block_copy(1).start()
     own.start()
     own_ids.start()
     for i in list(range(LEFT)) + list(range(LEFT + slab, wide)):
@@ -286,27 +294,36 @@
     own.wait()
     own_ids.wait()
 
+    ahead = wide - 1 - left_hops[-1][1] if depth > 1 else 1
     for hop in range(depth):
-        advance(PARTNERS, hop)
-        advance(0, hop)
-        if hop == min(1, depth - 1):
+        advance(PARTNERS, hop, 0)
+        if hop == depth - 1:
             open_block(1)
-    set_up()
-    lap_loop(0)
-    half = count // 2
-    advance(1, 0)
-    open_block(2)
-    field_loop(0, 0, half)
-    for hop in range(1, depth):
-        advance(1, hop)
-        advance(2, hop - 1)
-        if hop == 1:
-            field_loop(0, half, count)
-    lap_loop(1)
-    field_loop(1, 0, count)
-    advance(2, depth - 1)
-    lap_loop(2)
-    field_loop(2, 0, count)
+            set_up()
+            lap_loop(0, 1, ahead)
+        for sub in range(SUBS):
+            advance(0, hop, sub)
+    lap_loop(0, ahead, wide - 1)
+    bounds = [count * k // CHUNKS for k in range(CHUNKS + 1)]
+    for group in range(PARTNERS):
+        events = []
+        if group + 1 < PARTNERS:
+            for hop in range(depth - 1):
+                for sub in range(SUBS):
+                    events.append((hop, sub))
+        if not events:
+            field_loop(group, 0, count)
+            continue
+        for k in range(CHUNKS):
+            field_loop(group, bounds[k], bounds[k + 1])
+            for hop, sub in events[len(events) * k // CHUNKS : len(events) * (k + 1) // CHUNKS]:
+                advance(group + 1, hop, sub)
+            if k == CHUNKS // 2 - 1 and group + 2 < PARTNERS:
+                open_block(group + 2)
+        lap_loop(group + 1, 1, ahead)
+        for sub in range(SUBS):
+            advance(group + 1, depth - 1, sub)
+        lap_loop(group + 1, ahead, wide - 1)
 
     ones = jnp.ones((8, shape[1]), jnp.float32)
     rows = []
@@ -356,7 +373,8 @@
         block_copy(step).wait_send()
     for group in range(PARTNERS + 1):
         for hop in range(depth):
-            each(group, hop, leave)
+            for sub in range(SUBS if group < PARTNERS else 1):
+                each(group, hop, sub, leave)
 
 
 def shards(n_mode, n_space, modes, regions, stiffness, nonlinear, plan):
@@ -394,8 +412,8 @@
             pltpu.SemaphoreType.DMA((2,)),
             pltpu.SemaphoreType.DMA((PARTNERS,)),
             pltpu.SemaphoreType.DMA((PARTNERS,)),
-            pltpu.SemaphoreType.DMA((PARTNERS + 1, 2, depth)),
-            pltpu.SemaphoreType.DMA((PARTNERS + 1, 2, depth)),
+            pltpu.SemaphoreType.DMA((PARTNERS + 1, 2, depth, SUBS)),
+            pltpu.SemaphoreType.DMA((PARTNERS + 1, 2, depth, SUBS)),
             pltpu.SemaphoreType.DMA((n_space,)),
             pltpu.SemaphoreType.DMA((n_space,)),
         ],

time: 92.1 us -> 86.5 us (0.939)
  Pallas kernels: 83.9 us -> 78.3 us
    pallas_call x1, Pallas kernels: 83.9 us -> 78.3 us  [shards(): pl.pallas_call(functools.partial(kernel, n_mode, n_space, count, slab), o...]
where the time goes in v3:
time: 86.5 us; the launch traced here: 86.2 us
  Pallas kernels  78.3 us (91%)
  local copies, waits for them, and re-layouts  7.07 us (8%)
    pallas_call x1, Pallas kernels, shards(): pl.pallas_call(functools.partial(kernel, n_mode, n_space, count, slab), o...  78.3 us
    unnamed x8, local copies, waits for them, and re-layouts  7.07 us

profile of v3, /device:TPU:0, one launch (start us, length us, event | category | flops | bytes accessed | tf_op | source)
XLA Modules:
  0.0 86.2 jit_solution(1061381727607845189)
XLA Ops:
  0.0 0.8 copy.6.plan_ref
  0.8 0.8 add_convert_fusion.ids_ref
  1.6 0.0 copy-start
  1.6 1.0 %copy-done = bf16[16,2,64,128]{3,2,1,0:T(8,128)(2,1)S(1)} copy-done((bf16[16,2,64,128]{3,2,1,0:T(8,128)(2,1)S(1)}, bf16[16,2,64,128]{3,2,1,0:T(8,128)(2,1)}, u32[]{:S(2)}) %copy-start) | copy-done | bytes 524312
  2.7 0.0 copy-start.1
  2.7 0.7 copy-done.1
  3.3 0.0 copy-start.2
  3.3 0.7 copy-done.2
  4.0 78.3 %shard_map.55 = f32[16,3,2,64,128]{4,3,2,1,0:T(8,128)} custom-call(s32[16,3]{1,0:T(8,128)S(1)} %copy.6.plan_ref, f32[8]{0:T(128)S(1)} %copy-done.1, f32[8]{0:T(128)S(1)} %copy-done.2, bf16[16,2,64,128]{3,2,1,0:T(8,128)(2,1)S(1)} %copy-done, bf16[2,64,128]{2,1,0:T(8,128)(2,1)S(1)} %add_convert_fusion.ids_ref), custom_call_target="tpu_custom_call" | custom-call | tf_op jit(solution)/shard_map/pallas_call | solution.py:389
  82.3 4.0 %copy.8 = f32[16,3,2,64,128]{4,3,2,1,0:T(8,128)} copy(f32[16,3,2,64,128]{4,3,2,1,0:T(8,128)} %shard_map.55) | data formatting | bytes 6291456
Async XLA Ops:
  1.6 1.0 %copy-start = (bf16[16,2,64,128]{3,2,1,0:T(8,128)(2,1)S(1)}, bf16[16,2,64,128]{3,2,1,0:T(8,128)(2,1)}, u32[]{:S(2)}) copy-start(bf16[16,2,64,128]{3,2,1,0:T(8,128)(2,1)} %modes_ref.1) | copy-start | bytes 1572868
  2.7 0.7 copy-start.1
  3.3 0.7 copy-start.2
